TPU v7x, 32 devices: a whole 2x2x4 slice. The times are simulated.
32 devices in a mesh: frame: 4 (over x, core), fsdp: 8 (over z, y).
Axes of the slice: x: 2, y: 2, z: 4, core: 2. Of those that a mesh axis runs over, the one named last changes fastest.
Arguments:
- window: bfloat16 [4, 128, 5120], P('frame', 'fsdp'), may hold values from -6 to 6
- levels: int32 [4], P('frame'), may hold values from 0 to 15
- actions: int32 [4], P('frame'), may hold values from 0 to 15
- cache_len: int32 [1], replicated, may hold values from 128 to 1920
- level_table: float32 [16, 3, 5120], replicated, may hold values from -4 to 4
- action_table: float32 [16, 3, 5120], replicated, may hold values from -4 to 4
- w_qkv: bfloat16 [3, 5120, 4096], P(None, None, 'fsdp'), may hold values from -0.078125 to 0.078125
- w_out: bfloat16 [4096, 5120], P('fsdp'), may hold values from -0.09375 to 0.09375
- cache_keys: bfloat16 [2048, 4096], P('frame', 'fsdp'), may hold values from -220 to 220
- cache_values: bfloat16 [2048, 4096], P('frame', 'fsdp'), may hold values from -6 to 6
- fresh_frame: bfloat16 [128, 5120], P('fsdp'), may hold values from -6 to 6
Outputs:
- next_window: bfloat16 [4, 128, 5120], P('frame', 'fsdp')
- finished: bfloat16 [128, 5120], P('fsdp')
- new_cache_keys: bfloat16 [2048, 4096], P('frame', 'fsdp')
- new_cache_values: bfloat16 [2048, 4096], P('frame', 'fsdp')
Inputs may be any that keep to these rules, and one draw needn't show every extreme that they name: Rows of the cache from cache_len on are unused.
All inputs are finite; a program needn't handle non-finite values.
Results may differ from a plain program's by a relative error of at most 0.015.
The roundings to bfloat16 on the way count: a program that leaves them out, or rounds other values in their place, can miss the bound.
Values may be sent and summed in bfloat16 or wider, within the bound.
A program may use at most 128 MiB of HBM per device.

v0:
```python
import math

import jax
import jax.numpy as jnp
from jax import lax
from jax.sharding import PartitionSpec as P

HD = 128


EPS = 1e-06
NEG = -1e30


def passed_along(block, axis, distance):
    devices = range(lax.axis_size(axis))
    route = [(i - distance, i) for i in devices if i - distance in devices]
    return lax.ppermute(block, axis, route)


def spread_2(block, axis, source):
    block = jnp.where(lax.axis_index(axis) == source, block, jnp.zeros_like(block))
    return lax.psum(block, axis)


def lookup(table, picks):
    entries = table.shape[0]
    onehot = (picks[:, None] == jnp.arange(entries, dtype=jnp.int32)[None, :]).astype(jnp.float32)
    return jnp.einsum("fl,lcd->fcd", onehot, table, precision=lax.Precision.HIGHEST)


def split_heads(block, groups):
    return block.reshape(block.shape[0], groups, HD).transpose(1, 0, 2)


def attend(state, queries, keys, values, valid):
    peak, total, accum = state
    scores = jnp.einsum("gqd,gkd->gqk", queries, keys, preferred_element_type=jnp.float32) * (
        1.0 / math.sqrt(HD)
    )
    scores = jnp.where(valid[None, None, :], scores, NEG)
    newest = jnp.maximum(peak, jnp.max(scores, axis=-1))
    weights = jnp.where(valid[None, None, :], jnp.exp(scores - newest[..., None]), 0.0)
    carried = jnp.exp(peak - newest)
    total = total * carried + jnp.sum(weights, axis=-1)
    accum = accum * carried[..., None] + jnp.einsum(
        "gqk,gkd->gqd", weights.astype(jnp.bfloat16), values, preferred_element_type=jnp.float32
    )
    return (newest, total, accum)


def insert_rows(shard, fresh_rows, first, length):
    shard_rows, width = shard.shape
    frame_tokens = fresh_rows.shape[0]
    offset = jnp.clip(length - first, -frame_tokens, shard_rows)
    padding = jnp.zeros((shard_rows, width), shard.dtype)
    padded = jnp.concatenate([padding, fresh_rows, padding], 0)
    placed = lax.dynamic_slice_in_dim(padded, shard_rows - offset, shard_rows, 0)
    position = first + jnp.arange(shard_rows, dtype=jnp.int32)
    inside = (position >= length) & (position < length + frame_tokens)
    return jnp.where(inside[:, None], placed, shard)


def on_device(
    window,
    levels,
    actions,
    cache_len,
    level_table,
    action_table,
    w_qkv,
    w_out,
    cache_keys,
    cache_values,
    fresh_frame,
):
    slot = lax.axis_index("frame")
    slot_count = lax.axis_size("frame")
    condition = (lookup(level_table, levels) + lookup(action_table, actions))[0]
    base_rows = window[0].astype(jnp.float32)
    center = base_rows - jnp.mean(base_rows, axis=-1, keepdims=True)
    spread = jnp.mean(center * center, axis=-1, keepdims=True)
    normed = (center * lax.rsqrt(spread + EPS) * (1.0 + condition[1]) + condition[0]).astype(
        jnp.bfloat16
    )
    packed = jnp.einsum(
        "td,cde->tce",
        lax.all_gather(normed, "fsdp", axis=0, tiled=True),
        w_qkv,
        preferred_element_type=jnp.float32,
    ).astype(jnp.bfloat16)
    frame_tokens = packed.shape[0]
    width = packed.shape[2]
    groups = width // HD
    query_rows = packed[:, 0]
    key_own = packed[:, 1]
    value_own = packed[:, 2]
    query = split_heads(query_rows, groups)
    length = cache_len[0]
    shard_rows = cache_keys.shape[0]
    initial = (
        jnp.full((groups, frame_tokens), NEG, jnp.float32),
        jnp.zeros((groups, frame_tokens), jnp.float32),
        jnp.zeros((groups, frame_tokens, HD), jnp.float32),
    )
    everyone = lax.all_gather(query_rows[None], "frame", axis=0, tiled=True)
    local_keys = split_heads(cache_keys, groups)
    local_values = split_heads(cache_values, groups)
    local_valid = slot * shard_rows + jnp.arange(shard_rows, dtype=jnp.int32) < length

    def one_frame(rows_query):
        return attend(
            initial, split_heads(rows_query, groups), local_keys, local_values, local_valid
        )

    local_peak, local_total, local_accum = lax.map(one_frame, everyone)
    peaks = lax.pmax(local_peak, "frame")
    rescale = jnp.exp(local_peak - peaks)
    sums = (
        lax.psum_scatter(
            (local_total * rescale).astype(jnp.bfloat16), "frame", scatter_dimension=0, tiled=True
        ).astype(jnp.float32),
        lax.psum_scatter(
            (local_accum * rescale[..., None]).astype(jnp.bfloat16),
            "frame",
            scatter_dimension=0,
            tiled=True,
        ).astype(jnp.float32),
    )
    own_peak = lax.dynamic_index_in_dim(peaks, slot, 0, keepdims=False)
    state = (own_peak, sums[0][0], sums[1][0])
    pieces = (
        lax.all_gather(key_own[None], "frame", axis=0, tiled=True),
        lax.all_gather(value_own[None], "frame", axis=0, tiled=True),
    )
    count = pieces[0].shape[0]

    def advance(index, inner):
        keys = lax.dynamic_index_in_dim(pieces[0], index, 0, keepdims=False)
        values = lax.dynamic_index_in_dim(pieces[1], index, 0, keepdims=False)
        allowed = jnp.full((frame_tokens,), index <= slot)
        return attend(inner, query, split_heads(keys, groups), split_heads(values, groups), allowed)

    peak, total, accum = lax.fori_loop(0, count, advance, state)
    attended = (
        (accum / total[..., None])
        .astype(jnp.bfloat16)
        .transpose(1, 0, 2)
        .reshape(frame_tokens, width)
    )
    projection = lax.psum_scatter(
        jnp.dot(attended, w_out, preferred_element_type=jnp.float32).astype(jnp.bfloat16),
        "fsdp",
        scatter_dimension=0,
        tiled=True,
    ).astype(jnp.float32)
    updated = (base_rows + condition[2] * projection).astype(jnp.bfloat16)
    moved = passed_along(updated, "frame", -1)
    moved = jnp.where(slot == slot_count - 1, fresh_frame, moved)
    root_keys, root_values, finished = (
        spread_2(key_own, "frame", 0),
        spread_2(value_own, "frame", 0),
        spread_2(updated, "frame", 0),
    )
    first = slot * shard_rows
    new_keys = insert_rows(cache_keys, root_keys, first, length)
    new_values = insert_rows(cache_values, root_values, first, length)
    return (moved[None], finished, new_keys, new_values)


def solution(mesh):
    in_specs = (
        P("frame", "fsdp", None),
        P("frame"),
        P("frame"),
        P(),
        P(),
        P(),
        P(None, None, "fsdp"),
        P("fsdp", None),
        P("frame", "fsdp"),
        P("frame", "fsdp"),
        P("fsdp", None),
    )
    out_specs = (P("frame", "fsdp", None), P("fsdp", None), P("frame", "fsdp"), P("frame", "fsdp"))
    return jax.shard_map(
        on_device, mesh=mesh, in_specs=in_specs, out_specs=out_specs, check_vma=False
    )
```

profile of v0, /device:TPU:0, one launch (start us, length us, event | category | flops | bytes accessed | tf_op | source)
XLA Modules:
  0.0 235.9 jit_solution(2185599237842777008)
XLA Ops:
  8.7 0.4 fusion.51
  9.2 0.4 fusion.53
  9.7 0.2 convert_reduce_fusion
  9.9 0.2 fusion.42
  10.1 0.8 fusion.45
  11.1 0.2 copy.37
  11.3 0.3 copy.40
  11.6 0.2 copy.38
  11.8 0.3 copy.41
  12.1 43.5 %all-gather.5.cloned.1.call-done = bf16[128,5120]{1,0:T(8,128)(2,1)} async-done(((bf16[16,5120]{1,0:T(8,128)(2,1)}), bf16[128,5120]{1,0:T(8,128)(2,1)}) %all-gather.5.cloned.1.call-update) | async-done | bytes 1310736 | tf_op jit(solution)/shard_map/all_gather | solution.py:88
  55.6 8.1 %fusion.29 = bf16[128,3,512]{2,0,1:T(8,128)(2,1)S(1)} fusion(bf16[3,5120,512]{2,1,0:T(8,128)(2,1)} %param.21, bf16[128,5120]{1,0:T(8,128)(2,1)} %all-gather.5.cloned.1.call-done), kind=kOutput, calls=%fused_computation.44 | convolution fusion | flops 2013462528 | bytes 17432576 | tf_op jit(solution)/shard_map/td,cde->tce/dot_general | solution.py:86
  63.7 0.7 select_bitcast_fusion.1
  64.4 7.1 %all-gather = bf16[512,1,512]{2,0,1:T(8,128)(2,1)S(1)} all-gather(bf16[128,1,512]{2,0,1:T(8,128)(2,1)S(1)} %get-tuple-element.307), channel_id=2, replica_groups=mesh['frame'=4,'fsdp'=8] {'frame'}, dimensions={0}, use_global_device_ids=true | all-gather | bytes 655360 | tf_op jit(solution)/shard_map/all_gather | solution.py:106
  71.6 11.0 %while.33 = (s32[]{:T(128)}, f32[4,4,128]{2,1,0:T(4,128)S(1)}, f32[4,4,128]{2,1,0:T(4,128)S(1)}, f32[4,4,128,128]{3,2,1,0:T(8,128)}, bf16[4,128,512]{2,1,0:T(8,1...) while((s32[]{:T(128)}, f32[4,4,128]{2,1,0:T(4,128)S(1)}, ...), condition=%wide.region_5.6_spmd.clone, body=%wide.region_2.5_spmd.clone.sunk | while | flops 136646144 | bytes 5400705 | solution.py:116
  71.7 0.1 copy.67
  71.8 0.7 add_compare_fusion.2
  72.5 0.4 fusion.93
  72.9 0.3 fusion.94
  73.2 1.1 fusion.96
  74.5 0.1 copy.67
  74.6 0.7 add_compare_fusion.2
  75.3 0.4 fusion.93
  75.6 0.3 fusion.94
  76.0 1.1 fusion.96
  77.2 0.1 copy.67
  77.3 0.7 add_compare_fusion.2
  78.0 0.4 fusion.93
  78.4 0.3 fusion.94
  78.7 1.1 fusion.96
  79.9 0.1 copy.67
  80.1 0.7 add_compare_fusion.2
  80.8 0.4 fusion.93
  81.1 0.3 fusion.94
  81.5 1.1 fusion.96
  82.6 6.6 %pmax.7 = f32[4,4,128]{2,1,0:T(4,128)S(1)} all-reduce(f32[4,4,128]{2,1,0:T(4,128)S(1)} %get-tuple-element.188), channel_id=1, replica_groups=mesh['frame'=4,'fsdp'=8] {'frame'}, use_global_device_ids=true, to_apply=%region_6.7 | all-reduce | flops 2048 | bytes 16384 | tf_op jit(solution)/shard_map/pmax | solution.py:117
  89.2 2.4 multiply_convert_fusion
  91.7 0.6 dynamic-slice
  92.3 5.7 %all-reduce = bf16[4,4,128]{2,1,0:T(4,128)(2,1)S(1)} all-reduce(bf16[4,4,128]{2,1,0:T(4,128)(2,1)S(1)} %get-tuple-element.290), channel_id=5, replica_groups=mesh['frame'=4,'fsdp'=8] {'frame'}, use_global_device_ids=true, to_apply=%region_7.8.clone | all-reduce | flops 2048 | bytes 8192
  98.0 0.6 bitcast_convert_fusion.1
  98.6 6.9 %all-gather.1 = bf16[512,1,512]{2,0,1:T(8,128)(2,1)S(1)} all-gather(bf16[128,1,512]{2,0,1:T(8,128)(2,1)S(1)} %get-tuple-element.306), channel_id=3, replica_groups=mesh['frame'=4,'fsdp'=8] {'frame'}, dimensions={0}, use_global_device_ids=true | all-gather | bytes 655360 | tf_op jit(solution)/shard_map/all_gather | solution.py:133
  105.5 9.1 %all-gather.2 = bf16[512,1,512]{2,0,1:T(8,128)(2,1)S(1)} all-gather(bf16[128,1,512]{2,0,1:T(8,128)(2,1)S(1)} %get-tuple-element.305), channel_id=4, replica_groups=mesh['frame'=4,'fsdp'=8] {'frame'}, dimensions={0}, use_global_device_ids=true | all-gather | bytes 655360 | tf_op jit(solution)/shard_map/all_gather | solution.py:134
  114.6 0.9 bitcast_convert_fusion
  115.5 4.8 %while.32 = (s32[]{:T(128)}, f32[4,128]{1,0:T(4,128)S(1)}, f32[4,128]{1,0:T(4,128)S(1)}, f32[4,128,128]{2,1,0:T(8,128)S(1)}, s32[]{:T(128)}, /*index=5*/bf16[4,1...) while((s32[]{:T(128)}, f32[4,128]{1,0:T(4,128)S(1)}, ...), condition=%wide.region_12.13_spmd, body=%wide.region_9.12_spmd.sunk | while | flops 34276352 | bytes 3309685 | solution.py:144
  115.7 0.1 copy.63
  115.8 0.2 fusion.88
  116.3 0.1 copy.65
  116.4 0.3 convolution_add_fusion.3
  116.9 0.1 copy.63
  117.0 0.2 fusion.88
  117.5 0.1 copy.65
  117.6 0.3 convolution_add_fusion.3
  118.2 0.2 fusion.88
  118.8 0.3 convolution_add_fusion.3
  119.4 0.2 fusion.88
  120.0 0.3 convolution_add_fusion.3
  120.5 4.4 %convolution_convert_fusion = bf16[128,5120]{1,0:T(8,128)(2,1)} fusion(bf16[128,512]{0,1:T(8,128)(2,1)S(1)} %bitcast.159, bf16[512,5120]{1,0:T(8,128)(2,1)} %param.22), kind=kOutput, calls=%fused_computation.41 | convolution fusion | flops 671744000 | bytes 6684672 | tf_op jit(solution)/shard_map/dot_general | solution.py:152
  125.0 63.7 %reduce-scatter.5.cloned.1.call-done = bf16[16,5120]{1,0:T(8,128)(2,1)} async-done(((bf16[128,5120]{1,0:T(8,128)(2,1)}), bf16[16,5120]{1,0:T(8,128)(2,1)}) %reduce-scatter.5.cloned.1.call-update) | async-done | bytes 163856 | tf_op jit(solution)/shard_map/reduce_scatter | solution.py:151
  188.8 1.6 broadcast_select_fusion
  190.4 1.3 collective-permute-start
  192.4 1.3 collective-permute-done
  193.7 0.7 select_bitcast_fusion
  194.4 31.1 %all-reduce.4.cloned.1.call-done = (bf16[16,5120]{1,0:T(8,128)(2,1)}, bf16[128,512]{1,0:T(8,128)(2,1)}, bf16[128,512]{1,0:T(8,128)(2,1)}) async-done(((bf16[16,5120]{1,0:T(8,128)(2,1)}, bf16[128,512]{1,0:T(8,128)(2,1)}, bf16[128,512]{1,0:T(8,128)(2,1)}), (bf16[16,5120]{1,0:T(8,128)(2,1)}, bf16[128,512]{1,0:T(8,128)(2,1)}, bf16[128,512]{1,0:T(8,128)(2,1)})) %all-reduce.4.cloned.1.call-update) | async-done | bytes 426000 | tf_op jit(solution)/shard_map/psum | solution.py:23
  225.5 3.2 %fusion.37 = (bf16[512,512]{1,0:T(8,128)(2,1)}, bf16[512,512]{1,0:T(8,128)(2,1)}) fusion(bf16[512,512]{1,0:T(8,128)(2,1)S(1)} %copy-done.5, s32[]{:T(128)S(6)} %select_n.87, bf16[512,512]{1,0:T(8,128)(2,1)S(1)} %broadcast.131, bf16[128,512]{1,0:T(8,128)(2,1)} %get-tuple-element.285, pred[512]{0:T(512)(128)(4,1)S(1)} %fusion.50, ...), kind=kLoop, calls=%fused_computation.55 | loop fusion | flops 3670016 | bytes 2884100 | tf_op jit(solution)/shard_map/jit(_where)/select_n | solution.py:61
  228.7 0.7 copy.101
  (92 shorter events, 3.2 us)
Async XLA Ops:
  7.2 1.5 copy-start
  7.2 2.0 copy-start.6
  7.2 2.5 %copy-start.1 = (bf16[1,16,5120]{2,1,0:T(8,128)(2,1)S(1)}, bf16[1,16,5120]{2,1,0:T(8,128)(2,1)}, u32[]{:S(2)}) copy-start(bf16[1,16,5120]{2,1,0:T(8,128)(2,1)} %param.15) | copy-start | bytes 491524
  7.2 48.4 %all-gather.5.cloned.1.call-start = ((), (), s32[]{:S(2)}) async-start(), calls=%async_computation.2 | async-start | bytes 1474560 | tf_op jit(solution)/shard_map/all_gather | solution.py:88
  9.1 1.9 copy-start.2
  10.1 1.4 copy-start.4
  11.0 103.6 %reduce-scatter.3.cloned.1.call-start = ((), (), s32[]{:S(2)}) async-start(), calls=%async_computation.3 | async-start | bytes 655360 | tf_op jit(solution)/shard_map/reduce_scatter | solution.py:123
  82.6 9.1 %copy-start.9 = (u32[32]{0:T(128)S(1)}, u32[32]{0:T(128)}, u32[]{:S(2)}) copy-start(u32[32]{0:T(128)} %constant.117) | copy-start | bytes 388
  91.6 97.1 %reduce-scatter.5.cloned.1.call-start = ((), (), s32[]{:S(2)}) async-start(), calls=%async_computation.4 | async-start | bytes 1474560 | tf_op jit(solution)/shard_map/reduce_scatter | solution.py:151
  124.9 68.7 %copy-start.7 = (bf16[16,5120]{1,0:T(8,128)(2,1)S(1)}, bf16[16,5120]{1,0:T(8,128)(2,1)}, u32[]{:S(2)}) copy-start(bf16[16,5120]{1,0:T(8,128)(2,1)} %param.25) | copy-start | bytes 491524
  125.0 100.5 %copy-start.3 = (bf16[512,512]{1,0:T(8,128)(2,1)S(1)}, bf16[512,512]{1,0:T(8,128)(2,1)}, u32[]{:S(2)}) copy-start(bf16[512,512]{1,0:T(8,128)(2,1)} %param.23) | copy-start | bytes 1572868
  125.0 100.5 %copy-start.5 = (bf16[512,512]{1,0:T(8,128)(2,1)S(1)}, bf16[512,512]{1,0:T(8,128)(2,1)}, u32[]{:S(2)}) copy-start(bf16[512,512]{1,0:T(8,128)(2,1)} %param.24) | copy-start | bytes 1572868
  125.0 100.4 %all-reduce.4.cloned.1.call-start = ((), (), s32[]{:S(2)}) async-start(), calls=%async_computation.5 | async-start | bytes 851968 | tf_op jit(solution)/shard_map/psum | solution.py:23
  190.4 3.3 %collective-permute-start = (bf16[16,5120]{1,0:T(8,128)(2,1)S(1)}, bf16[16,5120]{1,0:T(8,128)(2,1)S(1)}, u32[]{:S(2)}, u32[]{:S(2)}) collective-permute-start(bf16[16,5120]{1,0:T(8,128)(2,1)S(1)} %get-tuple-element.289), channel_id=1, source_target_pairs={{8,0},{16,8},{24,16},{9,1},{17,9},{25,17},{10,2},{18,10},{26,18},{... | collective-permute-start | bytes 491528 | tf_op jit(solution)/shard_map/ppermute | solution.py:18
  225.5 3.2 %copy-start.8 = (bf16[16,5120]{1,0:T(8,128)(2,1)S(1)}, bf16[16,5120]{1,0:T(8,128)(2,1)}, u32[]{:S(2)}) copy-start(bf16[16,5120]{1,0:T(8,128)(2,1)} %get-tuple-element.498) | copy-start | bytes 491524
Sparse Core Ops, SparseCore 0:
  11.1 44.4 all-gather.4
  91.7 22.1 reduce-scatter.2
  125.1 63.6 reduce-scatter.4
  192.5 32.8 all-reduce.3
where the time goes:
time: 236 us
  waiting for transfers between devices  140 us (59%)
  blocking collectives  35.4 us (15%)
  matrix products  21.2 us (9%)
  between operations  16.2 us (7%)
  other arithmetic  15.8 us (7%)
  local copies, waits for them, and re-layouts  5.7 us (2%)
    reduce_scatter x1, waiting for transfers between devices, on_device(): lax.psum_scatter(jnp.dot(attended, w_out, preferred_element_type=jnp.floa...  63.7 us
    all_gather x1, waiting for transfers between devices, on_device(): lax.all_gather(normed, 'fsdp', axis=0, tiled=True)  43.5 us
    psum x1, waiting for transfers between devices, spread_2(): return lax.psum(block, axis)  31.1 us
    all_gather x1, blocking collectives, on_device(): lax.all_gather(value_own[None], 'frame', axis=0, tiled=True)  9.09 us
    dot_general x1, matrix products, on_device(): jnp.einsum('td,cde->tce', lax.all_gather(normed, 'fsdp', axis=0, tiled=Tr...  8.09 us
    all_gather x1, blocking collectives, on_device(): everyone = lax.all_gather(query_rows[None], 'frame', axis=0, tiled=True)  7.13 us
    all_gather x1, blocking collectives, on_device(): lax.all_gather(key_own[None], 'frame', axis=0, tiled=True)  6.88 us
    pmax x1, blocking collectives, on_device(): peaks = lax.pmax(local_peak, 'frame')  6.64 us
  transfers between devices with their start and end apart: 5, of which 4 were waited for; matrix products, arithmetic and copies ran while one was open for 1% of the time, Pallas kernels for 0%

commit v1 on v0

--- a/solution.py
+++ b/solution.py
@@ -1,8 +1,11 @@
+import functools
 import math
 
 import jax
 import jax.numpy as jnp
 from jax import lax
+from jax.experimental import pallas as pl
+from jax.experimental.pallas import tpu as pltpu
 from jax.sharding import PartitionSpec as P
 
 HD = 128
@@ -168,6 +171,612 @@
     return (moved[None], finished, new_keys, new_values)
 
 
+MESH = pl.DeviceIdType.MESH
+PAIR = 2
+VMEM_BYTES = 60 * 1024 * 1024
+
+
+def fused(
+    F,
+    N,
+    n,
+    window,
+    levels,
+    actions,
+    cache_len,
+    level_table,
+    action_table,
+    w_qkv,
+    w_out,
+    cache_keys,
+    cache_values,
+    fresh,
+    next_out,
+    fin_out,
+    nk_out,
+    nv_out,
+    lt_v,
+    at_v,
+    wq_v,
+    wo_v,
+    cache_v,
+    kc,
+    vc,
+    gath,
+    base_n,
+    gate_s,
+    gate_n,
+    acc,
+    qkv_s,
+    qkv_r,
+    kv_s,
+    k0v0,
+    att_s,
+    att_r,
+    part,
+    pair,
+    y_s,
+    y_r,
+    zs_r,
+    zs_l,
+    zr_r,
+    zr_l,
+    fin_s,
+    fin_r,
+    new_v,
+    loc,
+    wq_sem,
+    ag_send,
+    ag_recv,
+    ca_send,
+    ca_recv,
+    ba_send,
+    ba_recv,
+    qk_send,
+    qk_recv,
+    at_send,
+    at_recv,
+    k0_send,
+    k0_recv,
+    ys_sem,
+    yr_sem,
+    zsr_sem,
+    zsl_sem,
+    zrr_sem,
+    zrl_sem,
+    fi_send,
+    fi_recv,
+):
+    f = lax.axis_index("frame")
+    i = lax.axis_index("fsdp")
+    Y = PAIR
+    Z = N // Y
+    z = lax.div(i, Y)
+    y = lax.rem(i, Y)
+    T = window.shape[1]
+    D = window.shape[2]
+    Dc = D // n
+    FT = N * T
+    R = cache_keys.shape[0]
+    C = cache_keys.shape[1]
+
+    def copy(src, dst, ss, rs, frame, shard):
+        return pltpu.make_async_remote_copy(
+            src_ref=src,
+            dst_ref=dst,
+            send_sem=ss,
+            recv_sem=rs,
+            device_id=(frame, shard),
+            device_id_type=MESH,
+        )
+
+    right, left, across = i + Y, i - Y, z * Y + (1 - y)
+
+    def head_cols(h):
+        return pl.ds(pl.multiple_of(h * HD, HD), HD)
+
+    lt_copy = pltpu.make_async_copy(level_table, lt_v, loc.at[0])
+    at_copy = pltpu.make_async_copy(action_table, at_v, loc.at[1])
+    lt_copy.start()
+    at_copy.start()
+    wq_copies = [
+        pltpu.make_async_copy(
+            w_qkv.at[:, pl.ds(c * Dc, Dc), :], wq_v.at[:, pl.ds(c * Dc, Dc), :], wq_sem.at[c]
+        )
+        for c in range(n)
+    ]
+    later = [
+        pltpu.make_async_copy(w_out, wo_v, loc.at[2]),
+        pltpu.make_async_copy(cache_keys, cache_v.at[0], loc.at[3]),
+        pltpu.make_async_copy(cache_values, cache_v.at[1], loc.at[4]),
+        pltpu.make_async_copy(cache_keys.at[:, head_cols(f)], kc.at[f], loc.at[5]),
+        pltpu.make_async_copy(cache_values.at[:, head_cols(f)], vc.at[f], loc.at[6]),
+    ]
+
+    barrier = pltpu.get_barrier_semaphore()
+    for d in range(1, F):
+        pl.semaphore_signal(
+            barrier, inc=1, device_id=(lax.rem(f + d, F), i), device_id_type=MESH
+        )
+    pl.semaphore_signal(barrier, inc=1, device_id=(f, across), device_id_type=MESH)
+
+    @pl.when(z > 0)
+    def _():
+        pl.semaphore_signal(barrier, inc=1, device_id=(f, left), device_id_type=MESH)
+
+    @pl.when(z < Z - 1)
+    def _():
+        pl.semaphore_signal(barrier, inc=1, device_id=(f, right), device_id_type=MESH)
+
+    lt_copy.wait()
+    at_copy.wait()
+    for item in wq_copies:
+        item.start()
+    for item in later:
+        item.start()
+    condition = lt_v[levels[0]] + at_v[actions[0]]
+    rows = window[0].astype(jnp.float32)
+    center = rows - jnp.mean(rows, axis=-1, keepdims=True)
+    spread = jnp.mean(center * center, axis=-1, keepdims=True)
+    normed = (
+        center * lax.rsqrt(spread + EPS) * (1.0 + condition[1:2]) + condition[0:1]
+    ).astype(jnp.bfloat16)
+    gate_s[...] = condition[2:3]
+    for c in range(n):
+        gath[c, i] = normed[:, c * Dc : (c + 1) * Dc]
+
+    pl.semaphore_wait(barrier, F + jnp.minimum(z, 1) + jnp.minimum(Z - 1 - z, 1))
+
+    def ag(c, zs, way, target):
+        s = zs * Y + y
+        return copy(
+            gath.at[c, s], gath.at[c, s], ag_send.at[c, zs, way], ag_recv.at[c, s], f, target
+        )
+
+    def ag_wait(c, s):
+        copy(gath.at[c, s], gath.at[c, s], ag_send.at[c, 0, 0], ag_recv.at[c, s], f, across).wait_recv()
+
+    for c in range(n):
+
+        @pl.when(z < Z - 1)
+        def _():
+            ag(c, z, 0, right).start()
+
+        @pl.when(z > 0)
+        def _():
+            ag(c, z, 1, left).start()
+
+        ag(c, z, 2, across).start()
+
+    def cache_copy(which, d):
+        k = lax.rem(f + d, F)
+        src, dst = ((cache_keys, kc), (cache_values, vc))[which]
+        return copy(
+            src.at[:, head_cols(k)], dst.at[f], ca_send.at[which, d], ca_recv.at[which, f], k, i
+        )
+
+    def cache_arrival(which, d):
+        k = lax.rem(f + d, F)
+        dst = (kc, vc)[which]
+        copy(dst.at[k], dst.at[k], ca_send.at[which, d], ca_recv.at[which, k], k, i).wait_recv()
+
+    before = lax.rem(f + F - 1, F)
+    base_copies = [
+        copy(window.at[0], base_n, ba_send.at[0], ba_recv.at[0], before, i),
+        copy(gate_s, gate_n, ba_send.at[1], ba_recv.at[1], before, i),
+    ]
+    for which in range(2):
+        for d in range(1, F):
+            cache_copy(which, d).start()
+    for item in base_copies:
+        item.start()
+
+    def forward(c):
+        for h in range(1, Z):
+
+            @pl.when(z - h >= 0)
+            def _():
+                zs = z - h
+                ag_wait(c, zs * Y + y)
+
+                @pl.when(z < Z - 1)
+                def _():
+                    ag(c, zs, 0, right).start()
+
+                ag(c, zs, 2, across).start()
+
+            @pl.when(z + h < Z)
+            def _():
+                zs = z + h
+                ag_wait(c, zs * Y + y)
+
+                @pl.when(z > 0)
+                def _():
+                    ag(c, zs, 1, left).start()
+
+                ag(c, zs, 2, across).start()
+
+    def project(c):
+        for zs in range(Z):
+            ag_wait(c, zs * Y + (1 - y))
+        wq_copies[c].wait()
+        tokens = gath[c].reshape(FT, Dc)
+        for k in range(3):
+            product = jnp.dot(
+                tokens, wq_v[k, c * Dc : (c + 1) * Dc, :], preferred_element_type=jnp.float32
+            )
+            if c > 0:
+                product = product + acc[k]
+            if c < n - 1:
+                acc[k] = product
+            else:
+                rounded = product.astype(jnp.bfloat16)
+                for h in range(F):
+                    qkv_s[h, k] = rounded[:, h * HD : (h + 1) * HD]
+                if k > 0:
+                    kv_s[k - 1] = rounded
+
+    forward(0)
+    for c in range(n):
+        if c + 1 < n:
+            forward(c + 1)
+        project(c)
+
+    def qkv_copy(d):
+        k = lax.rem(f + d, F)
+        return copy(qkv_s.at[k], qkv_r.at[f], qk_send.at[d], qk_recv.at[f], k, i)
+
+    order = [d for d in range(F // 2, F)] + [d for d in range(1, F // 2)]
+    for d in order:
+        qkv_copy(d).start()
+    qkv_r[f] = qkv_s[f]
+    for item in later[3:]:
+        item.wait()
+    for d in range(1, F):
+        for which in range(2):
+            cache_arrival(which, d)
+    length = cache_len[0]
+    for d in order:
+        k = lax.rem(f + d, F)
+        copy(qkv_r.at[k], qkv_r.at[k], qk_send.at[d], qk_recv.at[k], k, i).wait_recv()
+
+    factor = 1.0 / math.sqrt(HD)
+    past_valid = lax.broadcasted_iota(jnp.int32, (1, F * R), 1) < length
+    dims = (((1,), (1,)), ((), ()))
+
+    def att_copy(d):
+        target = lax.rem(f + d, F)
+        a = lax.rem(target + 1, F)
+        return copy(
+            att_s.at[a], att_r.at[:, head_cols(f)], at_send.at[d], at_recv.at[f], target, i
+        )
+
+    for d in order + [0]:
+        a = lax.rem(f + d + 1, F)
+        queries = qkv_r[a, 0]
+        past = lax.dot_general(
+            queries, kc[...].reshape(F * R, HD), dims, preferred_element_type=jnp.float32
+        )
+        now = lax.dot_general(
+            queries, qkv_r[:, 1].reshape(F * FT, HD), dims, preferred_element_type=jnp.float32
+        )
+        past = jnp.where(past_valid, past * factor, NEG)
+        now_valid = lax.broadcasted_iota(jnp.int32, (1, F * FT), 1) < (a + 1) * FT
+        now = jnp.where(now_valid, now * factor, NEG)
+        peak = jnp.maximum(
+            jnp.max(past, axis=-1, keepdims=True), jnp.max(now, axis=-1, keepdims=True)
+        )
+        past = jnp.exp(past - peak)
+        now = jnp.exp(now - peak)
+        total = jnp.sum(past, axis=-1, keepdims=True) + jnp.sum(now, axis=-1, keepdims=True)
+        mixed = jnp.dot(
+            past.astype(jnp.bfloat16),
+            vc[...].reshape(F * R, HD),
+            preferred_element_type=jnp.float32,
+        ) + jnp.dot(
+            now.astype(jnp.bfloat16),
+            qkv_r[:, 2].reshape(F * FT, HD),
+            preferred_element_type=jnp.float32,
+        )
+        result = (mixed / total).astype(jnp.bfloat16)
+        if d == 0:
+            att_r[:, head_cols(f)] = result
+        else:
+            att_s[a] = result
+            att_copy(d).start()
+
+    def k0_copy(d):
+        return copy(kv_s, k0v0, k0_send.at[d], k0_recv.at[0], lax.rem(f + d, F), i)
+
+    @pl.when(f == 0)
+    def _():
+        for d in range(1, F):
+            k0_copy(d).start()
+        k0v0[...] = kv_s[...]
+
+    later[0].wait()
+    for d in order:
+        k = lax.rem(f + d, F)
+        cols = att_r.at[:, head_cols(k)]
+        copy(cols, cols, at_send.at[d], at_recv.at[k], k, i).wait_recv()
+
+    def y_copy(c):
+        return copy(y_s.at[c], y_r.at[c], ys_sem.at[c], yr_sem.at[c], f, across)
+
+    def right_copy(c, zd):
+        return copy(zs_r.at[c, zd], zr_r.at[c, zd], zsr_sem.at[c, zd], zrr_sem.at[c, zd], f, right)
+
+    def left_copy(c, zd):
+        return copy(zs_l.at[c, zd], zr_l.at[c, zd], zsl_sem.at[c, zd], zrl_sem.at[c, zd], f, left)
+
+    def fin_copy(c, d):
+        return copy(
+            fin_s.at[c], fin_r.at[c], fi_send.at[c, d], fi_recv.at[c], lax.rem(f + d, F), i
+        )
+
+    def multiply(c):
+        part[...] = jnp.dot(
+            att_r[...], wo_v[:, c * Dc : (c + 1) * Dc], preferred_element_type=jnp.float32
+        ).reshape(N, T, Dc)
+        for zd in range(Z):
+            y_s[c, zd] = part[zd * Y + (1 - y)].astype(jnp.bfloat16)
+        y_copy(c).start()
+        for zd in range(Z):
+            pair[c, zd] = part[zd * Y + y]
+
+    def add_pair(c):
+        y_copy(c).wait_recv()
+        pair[c] = pair[c] + y_r[c].astype(jnp.float32)
+
+    def line(c, k):
+        @pl.when(z == k)
+        def _():
+            for zd in range(Z - 1, k, -1):
+                value = pair[c, zd]
+                if k > 0:
+                    right_copy(c, zd).wait_recv()
+                    value = value + zr_r[c, zd].astype(jnp.float32)
+                zs_r[c, zd] = value.astype(jnp.bfloat16)
+                right_copy(c, zd).start()
+
+        @pl.when(z == Z - 1 - k)
+        def _():
+            for zd in range(Z - 1 - k):
+                value = pair[c, zd]
+                if k > 0:
+                    left_copy(c, zd).wait_recv()
+                    value = value + zr_l[c, zd].astype(jnp.float32)
+                zs_l[c, zd] = value.astype(jnp.bfloat16)
+                left_copy(c, zd).start()
+
+    def finish(c):
+        @pl.when(z > 0)
+        def _():
+            right_copy(c, z).wait_recv()
+            pair[c, z] = pair[c, z] + zr_r[c, z].astype(jnp.float32)
+
+        @pl.when(z < Z - 1)
+        def _():
+            left_copy(c, z).wait_recv()
+            pair[c, z] = pair[c, z] + zr_l[c, z].astype(jnp.float32)
+
+        cols = slice(c * Dc, (c + 1) * Dc)
+        updated = (base_n[:, cols].astype(jnp.float32) + gate_n[:, cols] * pair[c, z]).astype(
+            jnp.bfloat16
+        )
+
+        @pl.when(f < F - 1)
+        def _():
+            next_out[0, :, cols] = updated
+
+        @pl.when(f == F - 1)
+        def _():
+            fin_s[c] = updated
+            for d in range(1, F):
+                fin_copy(c, d).start()
+            fin_out[:, cols] = updated
+
+    new_copies = [
+        pltpu.make_async_copy(new_v.at[0], nk_out, loc.at[7]),
+        pltpu.make_async_copy(new_v.at[1], nv_out, loc.at[8]),
+    ]
+
+    def insert():
+        @pl.when(f != 0)
+        def _():
+            k0_copy(1).wait_recv()
+
+        row = lax.broadcasted_iota(jnp.int32, (R, FT), 0) + (f * R - length)
+        pick = jnp.where(row == lax.broadcasted_iota(jnp.int32, (R, FT), 1), 1.0, 0.0).astype(
+            jnp.bfloat16
+        )
+        position = lax.broadcasted_iota(jnp.int32, (R, C), 0) + (f * R - length)
+        inside = (position >= 0) & (position < FT)
+        for k in range(2):
+            later[1 + k].wait()
+            placed = jnp.dot(pick, k0v0[k], preferred_element_type=jnp.float32)
+            new_v[k] = jnp.where(inside, placed, cache_v[k].astype(jnp.float32)).astype(
+                jnp.bfloat16
+            )
+            new_copies[k].start()
+
+    @pl.when(f == F - 1)
+    def _():
+        next_out[0] = fresh[...]
+
+    for step in range(n + Z):
+        if step < n:
+            multiply(step)
+        if step == 0:
+            for item in base_copies:
+                item.wait_recv()
+        if 0 <= step - 1 < n:
+            add_pair(step - 1)
+        for k in range(Z - 1):
+            if 0 <= step - 1 - k < n:
+                line(step - 1 - k, k)
+        if step == n:
+            insert()
+        if 0 <= step - Z < n:
+            finish(step - Z)
+
+    @pl.when(f < F - 1)
+    def _():
+        for c in range(n):
+            fin_copy(c, 1).wait_recv()
+            fin_out[:, c * Dc : (c + 1) * Dc] = fin_r[c]
+
+    for c in range(n):
+        for zs in range(Z):
+
+            @pl.when((zs <= z) & (z < Z - 1))
+            def _():
+                ag(c, zs, 0, right).wait_send()
+
+            @pl.when((zs >= z) & (z > 0))
+            def _():
+                ag(c, zs, 1, left).wait_send()
+
+            ag(c, zs, 2, across).wait_send()
+
+            @pl.when(z < zs)
+            def _():
+                right_copy(c, zs).wait_send()
+
+            @pl.when(z > zs)
+            def _():
+                left_copy(c, zs).wait_send()
+
+        y_copy(c).wait_send()
+    for d in range(1, F):
+        for which in range(2):
+            cache_copy(which, d).wait_send()
+        qkv_copy(d).wait_send()
+        att_copy(d).wait_send()
+    for item in base_copies:
+        item.wait_send()
+
+    @pl.when(f == 0)
+    def _():
+        for d in range(1, F):
+            k0_copy(d).wait_send()
+
+    @pl.when(f == F - 1)
+    def _():
+        for c in range(n):
+            for d in range(1, F):
+                fin_copy(c, d).wait_send()
+
+    for item in new_copies:
+        item.wait()
+
+
+def pieces_of(width):
+    return next(k for k in (4, 5, 2, 1) if width % (k * HD) == 0)
+
+
+def fused_call(mesh, *args):
+    window, _, _, _, level_table, action_table, w_qkv, w_out, cache_keys, cache_values, _ = args
+    F, N = mesh.shape["frame"], mesh.shape["fsdp"]
+    T, D = window.shape[1:]
+    R, C = cache_keys.shape
+    FT = N * T
+    Z = N // PAIR
+    n = pieces_of(D)
+    Dc = D // n
+    bf, f32 = jnp.bfloat16, jnp.float32
+    vmem = pl.BlockSpec(memory_space=pltpu.VMEM)
+    smem = pl.BlockSpec(memory_space=pltpu.SMEM)
+    anys = pl.BlockSpec(memory_space=pl.ANY)
+    dma = pltpu.SemaphoreType.DMA
+    scratch = [
+        pltpu.VMEM(level_table.shape, f32),
+        pltpu.VMEM(action_table.shape, f32),
+        pltpu.VMEM(w_qkv.shape, bf),
+        pltpu.VMEM(w_out.shape, bf),
+        pltpu.VMEM((2, R, C), bf),
+        pltpu.VMEM((F, R, HD), bf),
+        pltpu.VMEM((F, R, HD), bf),
+        pltpu.VMEM((n, N, T, Dc), bf),
+        pltpu.VMEM((T, D), bf),
+        pltpu.VMEM((1, D), f32),
+        pltpu.VMEM((1, D), f32),
+        pltpu.VMEM((3, FT, C), f32),
+        pltpu.VMEM((F, 3, FT, HD), bf),
+        pltpu.VMEM((F, 3, FT, HD), bf),
+        pltpu.VMEM((2, FT, C), bf),
+        pltpu.VMEM((2, FT, C), bf),
+        pltpu.VMEM((F, FT, HD), bf),
+        pltpu.VMEM((FT, C), bf),
+        pltpu.VMEM((N, T, Dc), f32),
+        pltpu.VMEM((n, Z, T, Dc), f32),
+        pltpu.VMEM((n, Z, T, Dc), bf),
+        pltpu.VMEM((n, Z, T, Dc), bf),
+        pltpu.VMEM((n, Z, T, Dc), bf),
+        pltpu.VMEM((n, Z, T, Dc), bf),
+        pltpu.VMEM((n, Z, T, Dc), bf),
+        pltpu.VMEM((n, Z, T, Dc), bf),
+        pltpu.VMEM((n, T, Dc), bf),
+        pltpu.VMEM((n, T, Dc), bf),
+        pltpu.VMEM((2, R, C), bf),
+        dma((9,)),
+        dma((n,)),
+        dma((n, Z, 3)),
+        dma((n, N)),
+        dma((2, F)),
+        dma((2, F)),
+        dma((2,)),
+        dma((2,)),
+        dma((F,)),
+        dma((F,)),
+        dma((F,)),
+        dma((F,)),
+        dma((F,)),
+        dma((1,)),
+        dma((n,)),
+        dma((n,)),
+        dma((n, Z)),
+        dma((n, Z)),
+        dma((n, Z)),
+        dma((n, Z)),
+        dma((n, F)),
+        dma((n,)),
+    ]
+    return pl.pallas_call(
+        functools.partial(fused, F, N, n),
+        out_shape=(
+            jax.ShapeDtypeStruct(window.shape, bf),
+            jax.ShapeDtypeStruct(window.shape[1:], bf),
+            jax.ShapeDtypeStruct(cache_keys.shape, bf),
+            jax.ShapeDtypeStruct(cache_values.shape, bf),
+        ),
+        in_specs=[vmem, smem, smem, smem, anys, anys, anys, anys, anys, anys, vmem],
+        out_specs=(vmem, vmem, anys, anys),
+        scratch_shapes=scratch,
+        compiler_params=pltpu.CompilerParams(
+            collective_id=0, has_side_effects=True, vmem_limit_bytes=VMEM_BYTES
+        ),
+    )(*args)
+
+
+def dispatch(mesh, *args):
+    window, w_qkv, cache_keys = args[0], args[6], args[8]
+    F, N = mesh.shape["frame"], mesh.shape["fsdp"]
+    heads = w_qkv.shape[2] // HD
+    suits = (
+        tuple(mesh.axis_names) == ("frame", "fsdp")
+        and F > 1
+        and heads == F
+        and window.shape[0] == 1
+        and N % PAIR == 0
+        and window.shape[1] % 16 == 0
+        and cache_keys.shape[0] % 16 == 0
+    )
+    if suits:
+        return fused_call(mesh, *args)
+    return on_device(*args)
+
+
 def solution(mesh):
     in_specs = (
         P("frame", "fsdp", None),
@@ -184,5 +793,5 @@
     )
     out_specs = (P("frame", "fsdp", None), P("fsdp", None), P("frame", "fsdp"), P("frame", "fsdp"))
     return jax.shard_map(
-        on_device, mesh=mesh, in_specs=in_specs, out_specs=out_specs, check_vma=False
-    )
+        functools.partial(dispatch, mesh), mesh=mesh, in_specs=in_specs, out_specs=out_specs, check_vma=False
+    )

time: 236 us -> 82.4 us (0.35)
  waiting for transfers between devices: 140 us -> 0 us
  Pallas kernels: 0 us -> 66.6 us
  blocking collectives: 35.4 us -> 0 us
  matrix products: 21.2 us -> 0 us
  other arithmetic: 15.8 us -> 0 us
  between operations: 16.2 us -> 2.58 us
  local copies, waits for them, and re-layouts: 5.7 us -> 12.8 us
    pallas_call x0 -> x1, Pallas kernels: none -> 66.6 us  [fused_call(): pl.pallas_call(functools.partial(fused, F, N, n), out_shape=(jax.ShapeDty...]
    reduce_scatter x2 -> x0, waiting for transfers between devices: 63.7 us -> none  [the longest x1 63.7 us: on_device(): lax.psum_scatter(jnp.dot(attended, w_out, preferred_element_type=jnp.floa...]
    all_gather x1 -> x0, waiting for transfers between devices: 43.5 us -> none  [on_device(): lax.all_gather(normed, 'fsdp', axis=0, tiled=True)]
    psum x1 -> x0, waiting for transfers between devices: 31.1 us -> none  [spread_2(): return lax.psum(block, axis)]
    all_gather x3 -> x0, blocking collectives: 23.1 us -> none  [the longest x1 9.09 us: on_device(): lax.all_gather(value_own[None], 'frame', axis=0, tiled=True)]
    dot_general x20 -> x0, matrix products: 21.2 us -> none  [the longest x1 8.09 us: on_device(): jnp.einsum('td,cde->tce', lax.all_gather(normed, 'fsdp', axis=0, tiled=Tr...]
    unnamed x26 -> x6, local copies, waits for them, and re-layouts: 2.27 us -> 12.8 us
    pmax x1 -> x0, blocking collectives: 6.64 us -> none  [on_device(): peaks = lax.pmax(local_peak, 'frame')]
  transfers between devices with their start and end apart: 5 -> 0, of which waited for: 4 -> 0; matrix products, arithmetic and copies ran while one was open for 1% -> 0% of each run, Pallas kernels for 0% -> 0%
where the time goes in v1:
time: 82.4 us; the launch traced here: 82 us
  Pallas kernels  66.6 us (81%)
  local copies, waits for them, and re-layouts  12.8 us (16%)
  between operations  2.58 us (3%)
    pallas_call x1, Pallas kernels, fused_call(): pl.pallas_call(functools.partial(fused, F, N, n), out_shape=(jax.ShapeDty...  66.6 us
    unnamed x6, local copies, waits for them, and re-layouts  12.8 us

profile of v1, /device:TPU:0, one launch (start us, length us, event | category | flops | bytes accessed | tf_op | source)
XLA Modules:
  0.0 82.0 jit_solution(8486874770475221182)
XLA Ops:
  2.6 3.0 %copy.15.level_table = f32[16,3,5120]{2,1,0:T(4,128)} copy(f32[16,3,5120]{2,0,1:T(8,128)} %param.15) | data formatting | bytes 1966080 | tf_op args[4]
  5.5 3.0 %copy.16.action_table = f32[16,3,5120]{2,1,0:T(4,128)} copy(f32[16,3,5120]{2,0,1:T(8,128)} %param.16) | data formatting | bytes 1966080 | tf_op args[5]
  8.5 66.6 %shard_map.138 = (bf16[1,16,5120]{2,1,0:T(8,128)(2,1)}, bf16[16,5120]{1,0:T(8,128)(2,1)}, bf16[512,512]{1,0:T(8,128)(2,1)}, bf16[512,512]{1,0:T(8,128)(2,1)}) custom-call(bf16[1,16,5120]{2,1,0:T(8,128)(2,1)} %window.1, s32[1]{0:T(128)S(6)} %copy.21.levels, s32[1]{0:T(128)S(6)} %copy.22.actions, s32[1]{0:T(128)S(6)} %copy.23.cache_len, ...), custom_call_target="tpu_custom_call" | custom-call | tf_op jit(solution)/shard_map/pallas_call | solution.py:745
  75.1 1.6 %copy.24 = bf16[1,16,5120]{2,1,0:T(8,128)(2,1)} copy(bf16[1,16,5120]{2,1,0:T(8,128)(2,1)} %get-tuple-element.8) | data formatting | bytes 327680
  76.7 1.6 %copy.25 = bf16[16,5120]{1,0:T(8,128)(2,1)} copy(bf16[16,5120]{1,0:T(8,128)(2,1)} %get-tuple-element.9) | data formatting | bytes 327680
  78.3 1.9 %copy.26 = bf16[512,512]{1,0:T(8,128)(2,1)} copy(bf16[512,512]{1,0:T(8,128)(2,1)} %get-tuple-element.10) | data formatting | bytes 1048576
  80.1 1.9 %copy.27 = bf16[512,512]{1,0:T(8,128)(2,1)} copy(bf16[512,512]{1,0:T(8,128)(2,1)} %get-tuple-element.11) | data formatting | bytes 1048576

commit v2 on v1

--- a/solution.py
+++ b/solution.py
@@ -314,14 +314,15 @@
         item.start()
     for item in later:
         item.start()
-    condition = lt_v[levels[0]] + at_v[actions[0]]
+    level, action = levels[0], actions[0]
+    condition = [lt_v[k, pl.ds(level, 1), :] + at_v[k, pl.ds(action, 1), :] for k in range(3)]
     rows = window[0].astype(jnp.float32)
     center = rows - jnp.mean(rows, axis=-1, keepdims=True)
     spread = jnp.mean(center * center, axis=-1, keepdims=True)
     normed = (
-        center * lax.rsqrt(spread + EPS) * (1.0 + condition[1:2]) + condition[0:1]
+        center * lax.rsqrt(spread + EPS) * (1.0 + condition[1]) + condition[0]
     ).astype(jnp.bfloat16)
-    gate_s[...] = condition[2:3]
+    gate_s[...] = condition[2]
     for c in range(n):
         gath[c, i] = normed[:, c * Dc : (c + 1) * Dc]
 
@@ -440,7 +441,16 @@
         k = lax.rem(f + d, F)
         copy(qkv_r.at[k], qkv_r.at[k], qk_send.at[d], qk_recv.at[k], k, i).wait_recv()
 
-    factor = 1.0 / math.sqrt(HD)
+    def k0_copy(d):
+        return copy(kv_s, k0v0, k0_send.at[d], k0_recv.at[0], lax.rem(f + d, F), i)
+
+    @pl.when(f == 0)
+    def _():
+        for d in range(1, F):
+            k0_copy(d).start()
+        k0v0[...] = kv_s[...]
+
+    factor = math.log2(math.e) / math.sqrt(HD)
     past_valid = lax.broadcasted_iota(jnp.int32, (1, F * R), 1) < length
     dims = (((1,), (1,)), ((), ()))
 
@@ -451,23 +461,31 @@
             att_s.at[a], att_r.at[:, head_cols(f)], at_send.at[d], at_recv.at[f], target, i
         )
 
-    for d in order + [0]:
-        a = lax.rem(f + d + 1, F)
-        queries = qkv_r[a, 0]
+    everything = order + [0]
+    half = max(1, F // 2)
+    for group in [everything[at : at + half] for at in range(0, F, half)]:
+        frames = [lax.rem(f + d + 1, F) for d in group]
+        queries = jnp.concatenate([qkv_r[a, 0] for a in frames], 0)
         past = lax.dot_general(
             queries, kc[...].reshape(F * R, HD), dims, preferred_element_type=jnp.float32
         )
         now = lax.dot_general(
             queries, qkv_r[:, 1].reshape(F * FT, HD), dims, preferred_element_type=jnp.float32
         )
-        past = jnp.where(past_valid, past * factor, NEG)
-        now_valid = lax.broadcasted_iota(jnp.int32, (1, F * FT), 1) < (a + 1) * FT
-        now = jnp.where(now_valid, now * factor, NEG)
+        past = jnp.where(past_valid, past, NEG)
+        token = lax.broadcasted_iota(jnp.int32, (FT, F * FT), 1)
+        now = jnp.concatenate(
+            [
+                jnp.where(token < (a + 1) * FT, now[at * FT : (at + 1) * FT], NEG)
+                for at, a in enumerate(frames)
+            ],
+            0,
+        )
         peak = jnp.maximum(
             jnp.max(past, axis=-1, keepdims=True), jnp.max(now, axis=-1, keepdims=True)
         )
-        past = jnp.exp(past - peak)
-        now = jnp.exp(now - peak)
+        past = jnp.exp2((past - peak) * factor)
+        now = jnp.exp2((now - peak) * factor)
         total = jnp.sum(past, axis=-1, keepdims=True) + jnp.sum(now, axis=-1, keepdims=True)
         mixed = jnp.dot(
             past.astype(jnp.bfloat16),
@@ -479,21 +497,39 @@
             preferred_element_type=jnp.float32,
         )
         result = (mixed / total).astype(jnp.bfloat16)
-        if d == 0:
-            att_r[:, head_cols(f)] = result
-        else:
-            att_s[a] = result
-            att_copy(d).start()
-
-    def k0_copy(d):
-        return copy(kv_s, k0v0, k0_send.at[d], k0_recv.at[0], lax.rem(f + d, F), i)
-
-    @pl.when(f == 0)
-    def _():
-        for d in range(1, F):
-            k0_copy(d).start()
-        k0v0[...] = kv_s[...]
-
+        for at, d in enumerate(group):
+            own = result[at * FT : (at + 1) * FT]
+            if d == 0:
+                att_r[:, head_cols(f)] = own
+            else:
+                att_s[frames[at]] = own
+                att_copy(d).start()
+
+    new_copies = [
+        pltpu.make_async_copy(new_v.at[0], nk_out, loc.at[7]),
+        pltpu.make_async_copy(new_v.at[1], nv_out, loc.at[8]),
+    ]
+
+    def insert():
+        @pl.when(f != 0)
+        def _():
+            k0_copy(1).wait_recv()
+
+        row = lax.broadcasted_iota(jnp.int32, (R, FT), 0) + (f * R - length)
+        pick = jnp.where(row == lax.broadcasted_iota(jnp.int32, (R, FT), 1), 1.0, 0.0).astype(
+            jnp.bfloat16
+        )
+        position = lax.broadcasted_iota(jnp.int32, (R, C), 0) + (f * R - length)
+        inside = (position >= 0) & (position < FT)
+        for k in range(2):
+            later[1 + k].wait()
+            placed = jnp.dot(pick, k0v0[k], preferred_element_type=jnp.float32)
+            new_v[k] = jnp.where(inside, placed, cache_v[k].astype(jnp.float32)).astype(
+                jnp.bfloat16
+            )
+            new_copies[k].start()
+
+    insert()
     later[0].wait()
     for d in order:
         k = lax.rem(f + d, F)
@@ -575,30 +611,6 @@
             for d in range(1, F):
                 fin_copy(c, d).start()
             fin_out[:, cols] = updated
-
-    new_copies = [
-        pltpu.make_async_copy(new_v.at[0], nk_out, loc.at[7]),
-        pltpu.make_async_copy(new_v.at[1], nv_out, loc.at[8]),
-    ]
-
-    def insert():
-        @pl.when(f != 0)
-        def _():
-            k0_copy(1).wait_recv()
-
-        row = lax.broadcasted_iota(jnp.int32, (R, FT), 0) + (f * R - length)
-        pick = jnp.where(row == lax.broadcasted_iota(jnp.int32, (R, FT), 1), 1.0, 0.0).astype(
-            jnp.bfloat16
-        )
-        position = lax.broadcasted_iota(jnp.int32, (R, C), 0) + (f * R - length)
-        inside = (position >= 0) & (position < FT)
-        for k in range(2):
-            later[1 + k].wait()
-            placed = jnp.dot(pick, k0v0[k], preferred_element_type=jnp.float32)
-            new_v[k] = jnp.where(inside, placed, cache_v[k].astype(jnp.float32)).astype(
-                jnp.bfloat16
-            )
-            new_copies[k].start()
 
     @pl.when(f == F - 1)
     def _():
@@ -615,8 +627,6 @@
         for k in range(Z - 1):
             if 0 <= step - 1 - k < n:
                 line(step - 1 - k, k)
-        if step == n:
-            insert()
         if 0 <= step - Z < n:
             finish(step - Z)
 
@@ -671,11 +681,26 @@
         item.wait()
 
 
+def hand_out(*refs):
+    sources, targets, sems = refs[:4], refs[4:8], refs[8]
+    copies = [
+        pltpu.make_async_copy(source, target, sems.at[k])
+        for k, (source, target) in enumerate(zip(sources, targets))
+    ]
+    for item in copies:
+        item.start()
+    for item in copies:
+        item.wait()
+
+
 def pieces_of(width):
     return next(k for k in (4, 5, 2, 1) if width % (k * HD) == 0)
 
 
 def fused_call(mesh, *args):
+    args = list(args)
+    for at in (4, 5):
+        args[at] = args[at].transpose(1, 0, 2)
     window, _, _, _, level_table, action_table, w_qkv, w_out, cache_keys, cache_values, _ = args
     F, N = mesh.shape["frame"], mesh.shape["fsdp"]
     T, D = window.shape[1:]
@@ -742,7 +767,7 @@
         dma((n, F)),
         dma((n,)),
     ]
-    return pl.pallas_call(
+    results = pl.pallas_call(
         functools.partial(fused, F, N, n),
         out_shape=(
             jax.ShapeDtypeStruct(window.shape, bf),
@@ -757,6 +782,13 @@
             collective_id=0, has_side_effects=True, vmem_limit_bytes=VMEM_BYTES
         ),
     )(*args)
+    return pl.pallas_call(
+        hand_out,
+        out_shape=tuple(jax.ShapeDtypeStruct(r.shape, r.dtype) for r in results),
+        in_specs=[anys] * 4,
+        out_specs=(anys,) * 4,
+        scratch_shapes=[dma((4,))],
+    )(*results)
 
 
 def dispatch(mesh, *args):

time: 82.4 us -> 117 us (1.42)
  Pallas kernels: 66.6 us -> 114 us
  local copies, waits for them, and re-layouts: 12.8 us -> 0 us
    pallas_call x0 -> x1, Pallas kernels: none -> 42.8 us  [fused_call(): pl.pallas_call(hand_out, out_shape=tuple((jax.ShapeDtypeStruct(r.shape, r...]
    unnamed x6 -> x0, local copies, waits for them, and re-layouts: 12.8 us -> none
    pallas_call x1, Pallas kernels: 66.6 us -> 70.9 us  [fused_call(): pl.pallas_call(functools.partial(fused, F, N, n), out_shape=(jax.ShapeDty...]
where the time goes in v2:
time: 117 us; the launch traced here: 116 us
  Pallas kernels  114 us (97%)
  between operations  2.58 us (2%)
    pallas_call x1, Pallas kernels, fused_call(): pl.pallas_call(functools.partial(fused, F, N, n), out_shape=(jax.ShapeDty...  70.9 us
    pallas_call x1, Pallas kernels, fused_call(): pl.pallas_call(hand_out, out_shape=tuple((jax.ShapeDtypeStruct(r.shape, r...  42.8 us

profile of v2, /device:TPU:0, one launch (start us, length us, event | category | flops | bytes accessed | tf_op | source)
XLA Modules:
  0.0 116.3 jit_solution(2835181714145045536)
XLA Ops:
  2.6 70.9 %shard_map.138 = (bf16[1,16,5120]{2,1,0:T(8,128)(2,1)}, bf16[16,5120]{1,0:T(8,128)(2,1)}, bf16[512,512]{1,0:T(8,128)(2,1)}, bf16[512,512]{1,0:T(8,128)(2,1)}) custom-call(bf16[1,16,5120]{2,1,0:T(8,128)(2,1)} %window.1, s32[1]{0:T(128)S(6)} %copy.15.levels, s32[1]{0:T(128)S(6)} %copy.16.actions, s32[1]{0:T(128)S(6)} %copy.17.cache_len, ...), custom_call_target="tpu_custom_call" | custom-call | tf_op jit(solution)/shard_map/pallas_call | solution.py:770
  73.5 42.8 %shard_map.139 = (bf16[1,16,5120]{2,1,0:T(8,128)(2,1)}, bf16[16,5120]{1,0:T(8,128)(2,1)}, bf16[512,512]{1,0:T(8,128)(2,1)}, bf16[512,512]{1,0:T(8,128)(2,1)}) custom-call(bf16[1,16,5120]{2,1,0:T(8,128)(2,1)} %get-tuple-element.8.refs_0_, bf16[16,5120]{1,0:T(8,128)(2,1)} %get-tuple-element.9.refs_1_, bf16[512,512]{1,0:T(8,128)(2,1)} %get-tuple-element.10.refs_2_, ...), custom_call_target="tpu_custom_call" | custom-call | tf_op jit(solution)/shard_map/pallas_call | solution.py:785
